TPU v7x, 512 devices: a whole 4x4x16 slice. The times are simulated.
512 devices in a mesh: dp: 32 (over z, x_hi), vocab: 8 (over y, core), ends: 2 (over x_lo).
Axes of the slice: x: 4 (x_hi: 2, x_lo: 2; x = x_hi * 2 + x_lo), y: 4, z: 16, core: 2. Of those that a mesh axis runs over, the one named last changes fastest.
Arguments:
- hidden: bfloat16 [16384, 4608], P('dp', 'ends'), may hold values from -6 to 6
- cotangent: bfloat16 [16384, 4608], P('dp', 'ends'), may hold values from -0.09375 to 0.09375
- token_ids: int32 [16384], P('dp'), may hold values from 0 to 4095
- target_ids: int32 [16384], P('dp'), may hold values from 0 to 4095
- loss_mask: int32 [16384], P('dp'), may hold values 0 or 1
- embedding: bfloat16 [4096, 4608], P('vocab', 'ends'), may hold values from -0.375 to 0.375
Outputs:
- weight_grad: bfloat16 [8, 512, 4608], P('vocab', 'dp', 'ends')
All inputs are finite; a program needn't handle non-finite values. No bound on the sum of `loss_mask` on one device may be relied on, other than what follows from the above.
Results may differ from a plain program's by a relative error of at most 0.023.
Values may be sent and summed in bfloat16 or wider, within the bound.
A program may use at most 64 MiB of HBM per device.

v0:
```python
import math

import jax
import jax.numpy as jnp
from jax import lax
from jax.sharding import PartitionSpec as P

D = 4608


SOFTCAP = 30.0


def softmax_coeff(logits, targets, weight, first):
    shifted = jnp.exp(logits - SOFTCAP)
    total = lax.psum(jnp.sum(shifted, axis=1), "vocab")
    columns = first + lax.iota(jnp.int32, logits.shape[1])
    hit = (targets[:, None] == columns[None, :]).astype(jnp.float32)
    probs = shifted / total[:, None]
    return (weight[:, None] * (probs - hit) * (1.0 - (logits / SOFTCAP) ** 2)).astype(jnp.bfloat16)


def shards(hidden, cotangent, token_ids, target_ids, loss_mask, embedding):
    vocab_rows = embedding.shape[0]
    first = lax.axis_index("vocab") * vocab_rows
    weight = loss_mask.astype(jnp.float32)
    raw = lax.psum(
        lax.dot_general(
            hidden, embedding, (((1,), (1,)), ((), ())), preferred_element_type=jnp.float32
        ),
        "ends",
    )
    logits = SOFTCAP * jnp.tanh(raw / SOFTCAP)
    coeff = softmax_coeff(logits, target_ids, weight, first)
    normalizer = jnp.asarray(math.sqrt(D), jnp.float32).astype(jnp.bfloat16)
    columns = first + lax.iota(jnp.int32, vocab_rows)
    picks = jnp.where(
        token_ids[:, None] == columns[None, :], normalizer, jnp.zeros((), jnp.bfloat16)
    )
    head = lax.dot_general(
        coeff, hidden, (((0,), (0,)), ((), ())), preferred_element_type=jnp.float32
    )
    embed = lax.dot_general(
        picks, cotangent, (((0,), (0,)), ((), ())), preferred_element_type=jnp.float32
    )
    summed = lax.psum_scatter(
        (head + embed).astype(jnp.bfloat16), "dp", scatter_dimension=0, tiled=True
    )
    return summed[None]


def solution(mesh):
    return jax.shard_map(
        shards,
        mesh=mesh,
        in_specs=(P("dp", "ends"), P("dp", "ends"), P("dp"), P("dp"), P("dp"), P("vocab", "ends")),
        out_specs=P("vocab", "dp", "ends"),
        check_vma=False,
    )
```

profile of v0, /device:TPU:8, one launch (start us, length us, event | category | flops | bytes accessed | tf_op | source)
XLA Modules:
  0.0 777.2 jit_solution(8814133264618407702)
XLA Ops:
  6.5 0.0 copy-start
  6.5 0.0 copy-start.1
  6.5 0.0 copy-start.3
  6.5 0.0 all-reduce.2.cloned.1.call-start
  6.5 1.7 copy-done
  8.2 4.1 fusion.21
  12.3 0.0 all-reduce.2.cloned.1.call-update
  12.3 0.0 reduce-scatter.2.cloned.1.call-start
  12.4 0.0 copy-done.1
  12.4 66.5 %all-reduce.2.cloned.1.call-done = f32[512,512]{1,0:T(8,128)} async-done(((f32[512,512]{1,0:T(8,128)}), f32[512,512]{1,0:T(8,128)}) %all-reduce.2.cloned.1.call-update) | async-done | bytes 1048592 | tf_op jit(solution)/shard_map/psum | solution.py:27
  78.9 1.6 fusion.1
  80.5 11.7 %psum.15 = f32[512]{0:T(512)S(1)} all-reduce(f32[512]{0:T(512)S(1)} %fusion.1), channel_id=1, replica_groups=mesh['dp'=32,'vocab'=8,'ends'=2] {'vocab'}, use_global_device_ids=true, to_apply=%region_2.0 | all-reduce | flops 512 | bytes 4096 | tf_op jit(solution)/shard_map/psum | solution.py:16
  92.2 0.0 copy-done.3
  92.2 0.0 copy-start.2
  92.2 0.0 copy-start.4
  92.2 3.1 fusion.2
  95.3 0.0 copy-done.2
  95.3 0.0 copy-done.4
  95.3 3.1 fusion
  98.3 0.0 reduce-scatter.2.cloned.1.call-update
  98.4 672.0 %reduce-scatter.2.cloned.1.call-done = bf16[16,2304]{1,0:T(8,128)(2,1)} async-done(((bf16[512,2304]{1,0:T(8,128)(2,1)}), bf16[16,2304]{1,0:T(8,128)(2,1)}) %reduce-scatter.2.cloned.1.call-update) | async-done | bytes 73744 | tf_op jit(solution)/shard_map/reduce_scatter | solution.py:46
  (2 shorter events, 0.0 us)
Async XLA Ops:
  6.5 1.7 copy-start
  6.5 5.9 copy-start.1
  6.5 85.6 %copy-start.3 = (s32[512]{0:T(512)S(1)}, s32[512]{0:T(512)}, u32[]{:S(2)}) copy-start(s32[512]{0:T(512)} %param.9) | copy-start | bytes 6148
  6.5 72.4 %all-reduce.2.cloned.1.call-start = ((), (), s32[]{:S(2)}) async-start(), calls=%async_computation.1 | async-start | bytes 2097152 | tf_op jit(solution)/shard_map/psum | solution.py:27
  12.3 758.1 %reduce-scatter.2.cloned.1.call-start = ((), (), s32[]{:S(2)}) async-start(), calls=%async_computation.2 | async-start | bytes 2433024 | tf_op jit(solution)/shard_map/reduce_scatter | solution.py:46
  92.2 3.1 copy-start.2
  92.2 3.1 copy-start.4
Sparse Core Ops, SparseCore 0:
  12.5 66.4 all-reduce.1
  98.5 671.8 reduce-scatter.1
where the time goes:
time: 777 us
  waiting for transfers between devices  739 us (95%)
  between operations  13.5 us (2%)
  blocking collectives  11.7 us (2%)
  matrix products  10.2 us (1%)
    reduce_scatter x1, waiting for transfers between devices, shards(): lax.psum_scatter((head + embed).astype(jnp.bfloat16), 'dp', scatter_dimen...  672 us
    psum x1, waiting for transfers between devices, shards(): lax.psum(lax.dot_general(hidden, embedding, (((1,), (1,)), ((), ())), pre...  66.5 us
  transfers between devices with their start and end apart: 2, of which 2 were waited for; matrix products, arithmetic and copies ran while one was open for 0% of the time, Pallas kernels for 0%

commit v1 on v0

v1 whole, which is shorter than its diff:
```python
import functools
import math

import jax
import jax.numpy as jnp
from jax import lax
from jax.experimental import pallas as pl
from jax.experimental.pallas import tpu as pltpu
from jax.sharding import PartitionSpec as P

D = 4608
SOFTCAP = 30.0
MESH = pl.DeviceIdType.MESH
F32 = jnp.float32
BF16 = jnp.bfloat16
PART = 16
CHUNK = 2 * PART
SUBS = 4


def dot_nt(a, b):
    return lax.dot_general(a, b, (((1,), (1,)), ((), ())), preferred_element_type=F32)


def dot_nn(a, b):
    return lax.dot_general(a, b, (((1,), (0,)), ((), ())), preferred_element_type=F32)


def rows_of(start, size):
    return pl.ds(pl.multiple_of(start, size), size)


def kernel(
    nz, nv, subs,
    hidden, cotangent, embedding, tokens, targets, mask,
    out,
    hid, cot, emb, raw_out, raw_in, own, tanhs, shifted, tot_out, tot_in, coeff, embed,
    part_out, part_in, *rest,
):
    n_subs = len(subs)
    bufs, sems = rest[: 3 * n_subs], rest[3 * n_subs :]
    send, recv, last = bufs[:n_subs], bufs[n_subs : 2 * n_subs], bufs[2 * n_subs :]
    load, raw_s, raw_r, tot_s, tot_r, ag_s, ag_r, ring_s, ring_r, last_s, last_r, part_s, part_r = sems

    d, v, e = lax.axis_index("dp"), lax.axis_index("vocab"), lax.axis_index("ends")
    z, h = d // 2, d % 2
    steps = nz // 2
    rows, half = own.shape
    width = hid.shape[2]

    def at_z(k, other):
        return (lax.rem(z + k + nz, nz) * 2 + (1 - h if other else h), v, e)

    mate = (d, v, 1 - e)
    cross = (z * 2 + 1 - h, v, e)
    ahead = (1, -1)

    barrier = pltpu.get_barrier_semaphore()
    greet = [mate, cross] + [at_z(k, o) for k in ahead for o in (False, True)]
    greet += [(d, lax.rem(v + o, nv), e) for o in range(1, nv)]
    for who in greet:
        pl.semaphore_signal(barrier, inc=1, device_id=who, device_id_type=MESH)

    quarter = rows // 4
    other_tokens, own_tokens = rows_of((1 - e) * half, half), rows_of(e * half, half)
    loads = [pltpu.make_async_copy(hidden.at[other_tokens], hid.at[1], load.at[0])]
    loads += [
        pltpu.make_async_copy(embedding.at[pl.ds(c * quarter, quarter)], emb.at[pl.ds(c * quarter, quarter)], load.at[1 + c])
        for c in range(4)
    ]
    loads += [
        pltpu.make_async_copy(hidden.at[own_tokens], hid.at[0], load.at[5]),
        pltpu.make_async_copy(cotangent, cot, load.at[6]),
    ]
    for copy in loads:
        copy.start()

    def raw_copy(c):
        block = rows_of(c * quarter, quarter)
        return pltpu.make_async_remote_copy(
            src_ref=raw_out.at[block], dst_ref=raw_in.at[block], send_sem=raw_s.at[c], recv_sem=raw_r.at[c],
            device_id=mate, device_id_type=MESH,
        )

    loads[0].wait()
    for c in range(4):
        loads[1 + c].wait()
        block = pl.ds(c * quarter, quarter)
        raw_out[block] = dot_nt(emb[block], hid[1]).astype(BF16)
        if c == 0:
            pl.semaphore_wait(barrier, len(greet))
        raw_copy(c).start()

    loads[5].wait()

    def own_block(c, _):
        block = rows_of(c * quarter, quarter)
        own[block] = dot_nt(emb[block], hid[0])
        return 0

    lax.fori_loop(0, 4, own_block, 0)

    loads[6].wait()
    normalizer = jnp.asarray(math.sqrt(D), F32).astype(BF16)
    first = v * rows

    def embed_block(c, _):
        block = rows_of(c * quarter, quarter)
        index = lax.broadcasted_iota(jnp.int32, (quarter, 2 * half), 0) + (first + c * quarter)
        picks = jnp.where(tokens[...] == index, normalizer.astype(F32), 0.0).astype(BF16)
        third = width // 3 if width % 384 == 0 else width
        for n in range(0, width, third):
            embed[block, pl.ds(n, third)] = dot_nn(picks, cot[:, pl.ds(n, third)])
        return 0

    lax.fori_loop(0, 4, embed_block, 0)

    def soft_block(c, total):
        block = rows_of(c * quarter, quarter)
        raw_copy(c).wait_recv()
        t = jnp.tanh((own[block] + raw_in[block].astype(F32)) * (1.0 / SOFTCAP))
        s = jnp.exp(t * SOFTCAP - SOFTCAP)
        tanhs[block] = t
        shifted[block] = s
        return total + jnp.sum(s, axis=0, keepdims=True)

    total = lax.fori_loop(0, 4, soft_block, jnp.zeros((1, half), F32))
    tot_out[...] = total

    def tot_copy(o, source):
        return pltpu.make_async_remote_copy(
            src_ref=tot_out, dst_ref=tot_in.at[source], send_sem=tot_s.at[o], recv_sem=tot_r.at[source],
            device_id=(d, lax.rem(v + o, nv), e), device_id_type=MESH,
        )

    for o in range(1, nv):
        tot_copy(o, v).start()
    for o in range(1, nv):
        source = lax.rem(v + o, nv)
        tot_copy(o, source).wait_recv()
        total = total + tot_in[source]
    weight = mask[e].astype(F32)
    target = targets[e]
    inverse = 1.0 / total

    def chunk_at(i):
        s, direction = i // 2, i % 2
        return lax.rem(z + jnp.where(direction == 0, steps - s, steps + s), nz)

    def ag_copy(i):
        block = rows_of(chunk_at(i) * CHUNK, CHUNK)
        return pltpu.make_async_remote_copy(
            src_ref=coeff.at[0, block], dst_ref=coeff.at[1, block], send_sem=ag_s.at[i], recv_sem=ag_r.at[i],
            device_id=mate, device_id_type=MESH,
        )

    def coeff_block(j, _):
        i = jnp.where(j == 0, 0, j + 1)
        start = chunk_at(i) * CHUNK
        block = rows_of(start, CHUNK)
        index = lax.broadcasted_iota(jnp.int32, (CHUNK, half), 0) + (first + start)
        hit = jnp.where(target == index, 1.0, 0.0)
        t = tanhs[block]
        coeff[0, block] = (weight * (shifted[block] * inverse - hit) * (1.0 - t * t)).astype(BF16)
        ag_copy(i).start()
        return 0

    lax.fori_loop(0, nz, coeff_block, 0)

    def partial_sums(chunks, c0, w):
        blocks = [rows_of(c * CHUNK, CHUNK) for c in chunks]
        cols = pl.ds(c0, w)
        got = embed[blocks[0], cols] if len(blocks) == 1 else jnp.concatenate([embed[b, cols] for b in blocks], axis=0)
        for k in (0, 1):
            left = coeff[k, blocks[0]] if len(blocks) == 1 else jnp.concatenate([coeff[k, b] for b in blocks], axis=0)
            got = got + dot_nn(left, hid[k, :, cols])
        return got

    def ring_copy(direction, u, s):
        return pltpu.make_async_remote_copy(
            src_ref=send[u].at[direction, s], dst_ref=recv[u].at[direction, s],
            send_sem=ring_s.at[direction, u, s], recv_sem=ring_r.at[direction, u, s],
            device_id=at_z(ahead[direction], False), device_id_type=MESH,
        )

    def last_copy(direction, u, other):
        target_h = 1 - h if other else h
        return pltpu.make_async_remote_copy(
            src_ref=send[u].at[direction, steps - 1, rows_of(target_h * PART, PART)],
            dst_ref=last[u].at[direction, h],
            send_sem=last_s.at[direction, u, int(other)], recv_sem=last_r.at[direction, u, h],
            device_id=at_z(ahead[direction], other), device_id_type=MESH,
        )

    def last_wait(direction, u, source):
        pltpu.make_async_remote_copy(
            src_ref=send[u].at[direction, steps - 1, pl.ds(0, PART)],
            dst_ref=last[u].at[direction, source],
            send_sem=last_s.at[direction, u, 0], recv_sem=last_r.at[direction, u, source],
            device_id=at_z(ahead[direction], False), device_id_type=MESH,
        ).wait_recv()

    part_copy = pltpu.make_async_remote_copy(
        src_ref=part_out.at[rows_of((1 - h) * PART, PART)], dst_ref=part_in, send_sem=part_s, recv_sem=part_r,
        device_id=cross, device_id_type=MESH,
    )

    ag_copy(0).wait_recv()
    for u, (c0, w) in enumerate(subs):
        send[u][u % 2, 0] = partial_sums([chunk_at(0)], c0, w).astype(BF16)
        ring_copy(u % 2, u, 0).start()

    def ring_step(s, _):
        for i in (0, 1):
            ag_copy(2 * s + i).wait_recv()
        for u, (c0, w) in enumerate(subs):
            local = partial_sums([chunk_at(2 * s), chunk_at(2 * s + 1)], c0, w)
            for direction in (0, 1):
                mine = local[direction * CHUNK : (direction + 1) * CHUNK]
                if direction == u % 2:
                    ring_copy(direction, u, s - 1).wait_recv()
                    send[u][direction, s] = (mine + recv[u][direction, s - 1].astype(F32)).astype(BF16)
                else:
                    @pl.when(s == 1)
                    def _():
                        send[u][direction, s] = mine.astype(BF16)

                    @pl.when(s > 1)
                    def _():
                        ring_copy(direction, u, s - 1).wait_recv()
                        send[u][direction, s] = (mine + recv[u][direction, s - 1].astype(F32)).astype(BF16)

                @pl.when(s < steps - 1)
                def _():
                    ring_copy(direction, u, s).start()

                @pl.when(s == steps - 1)
                def _():
                    last_copy(direction, u, True).start()
                    last_copy(direction, u, False).start()
        return 0

    lax.fori_loop(1, steps, ring_step, 0)

    ag_copy(2 * steps).wait_recv()
    mine = []
    for u, (c0, w) in enumerate(subs):
        local = partial_sums([z], c0, w)
        part_out[:, pl.ds(c0, w)] = local.astype(BF16)
    part_copy.start()
    part_copy.wait_recv()
    for u, (c0, w) in enumerate(subs):
        for direction in (0, 1):
            for source in (0, 1):
                last_wait(direction, u, source)
        cols = pl.ds(c0, w)
        got = part_out[rows_of(h * PART, PART), cols].astype(F32) + part_in[:, cols].astype(F32)
        for direction in (0, 1):
            for source in (0, 1):
                got = got + last[u][direction, source].astype(F32)
        out[:, cols] = got.astype(BF16)

    for c in range(4):
        raw_copy(c).wait_send()
    for o in range(1, nv):
        tot_copy(o, v).wait_send()
    ag_copy(0).wait_send()

    def ag_done(i, _):
        ag_copy(i).wait_send()
        return 0

    lax.fori_loop(2, 2 * steps + 1, ag_done, 0)
    part_copy.wait_send()
    for u in range(n_subs):
        for direction in (0, 1):
            def ring_done(s, _):
                ring_copy(direction, u, s).wait_send()
                return 0

            lax.fori_loop(0 if direction == u % 2 else 1, steps - 1, ring_done, 0)
            for other in (True, False):
                last_copy(direction, u, other).wait_send()


def solution(mesh):
    nz, nv = mesh.shape["dp"] // 2, mesh.shape["vocab"]

    def shards(hidden, cotangent, token_ids, target_ids, loss_mask, embedding):
        tokens, width = hidden.shape
        rows = embedding.shape[0]
        half = tokens // 2
        steps = nz // 2
        ends = [width // 128 * i // SUBS * 128 for i in range(SUBS + 1)]
        subs = tuple((lo, hi - lo) for lo, hi in zip(ends, ends[1:]))
        any_space = pl.BlockSpec(memory_space=pl.ANY)
        in_vmem = pl.BlockSpec(memory_space=pltpu.VMEM)
        dma = pltpu.SemaphoreType.DMA
        scratch = [
            pltpu.VMEM((2, half, width), BF16),
            pltpu.VMEM((tokens, width), BF16),
            pltpu.VMEM((rows, width), BF16),
            pltpu.VMEM((rows, half), BF16),
            pltpu.VMEM((rows, half), BF16),
            pltpu.VMEM((rows, half), F32),
            pltpu.VMEM((rows, half), F32),
            pltpu.VMEM((rows, half), F32),
            pltpu.VMEM((1, half), F32),
            pltpu.VMEM((nv, 1, half), F32),
            pltpu.VMEM((2, rows, half), BF16),
            pltpu.VMEM((rows, width), F32),
            pltpu.VMEM((CHUNK, width), BF16),
            pltpu.VMEM((PART, width), BF16),
        ]
        scratch += [pltpu.VMEM((2, steps, CHUNK, w), BF16) for _, w in subs]
        scratch += [pltpu.VMEM((2, steps, CHUNK, w), BF16) for _, w in subs]
        scratch += [pltpu.VMEM((2, 2, PART, w), BF16) for _, w in subs]
        scratch += [
            dma((7,)), dma((4,)), dma((4,)), dma((nv,)), dma((nv,)),
            dma((2 * steps + 1,)), dma((2 * steps + 1,)),
            dma((2, SUBS, steps)), dma((2, SUBS, steps)), dma((2, SUBS, 2)), dma((2, SUBS, 2)), dma, dma,
        ]
        got = pl.pallas_call(
            functools.partial(kernel, nz, nv, subs),
            out_shape=jax.ShapeDtypeStruct((rows // (2 * nz), width), BF16),
            in_specs=[any_space] * 3 + [in_vmem] * 3,
            out_specs=in_vmem,
            scratch_shapes=scratch,
            compiler_params=pltpu.CompilerParams(
                collective_id=0, has_side_effects=True, vmem_limit_bytes=48 * 2**20
            ),
        )(
            hidden, cotangent, embedding,
            token_ids.reshape(1, tokens), target_ids.reshape(2, 1, half), loss_mask.reshape(2, 1, half),
        )
        return got[None]

    return jax.shard_map(
        shards,
        mesh=mesh,
        in_specs=(P("dp", "ends"), P("dp", "ends"), P("dp"), P("dp"), P("dp"), P("vocab", "ends")),
        out_specs=P("vocab", "dp", "ends"),
        check_vma=False,
    )
```

time: 777 us -> 67.2 us (0.09)
  the two profiles are of different devices: /device:TPU:8 before, /device:TPU:2 now
where the time goes in v1:
time: 67.2 us; the launch traced here: 67 us
  Pallas kernels  60.9 us (91%)
  local copies, waits for them, and re-layouts  6.01 us (9%)
    pallas_call x1, Pallas kernels, shards(): pl.pallas_call(functools.partial(kernel, nz, nv, subs), out_shape=jax.Sha...  60.9 us
    unnamed x11, local copies, waits for them, and re-layouts  6.01 us

profile of v1, /device:TPU:2, one launch (start us, length us, event | category | flops | bytes accessed | tf_op | source)
XLA Modules:
  0.0 67.0 jit_solution(12848757916997109574)
XLA Ops:
  0.0 0.0 copy-start
  0.0 1.7 %copy-done = bf16[512,2304]{1,0:T(8,128)(2,1)S(1)} copy-done((bf16[512,2304]{1,0:T(8,128)(2,1)S(1)}, bf16[512,2304]{1,0:T(8,128)(2,1)}, u32[]{:S(2)}) %copy-start) | copy-done | bytes 2359320
  1.7 0.0 copy-start.1
  1.7 1.7 %copy-done.1 = bf16[512,2304]{1,0:T(8,128)(2,1)S(1)} copy-done((bf16[512,2304]{1,0:T(8,128)(2,1)S(1)}, bf16[512,2304]{1,0:T(8,128)(2,1)}, u32[]{:S(2)}) %copy-start.1) | copy-done | bytes 2359320
  3.3 0.0 copy-start.2
  3.3 0.7 %copy-done.2 = s32[512]{0:T(512)S(1)} copy-done((s32[512]{0:T(512)S(1)}, s32[512]{0:T(512)}, u32[]{:S(2)}) %copy-start.2) | copy-done | bytes 2072
  4.0 0.0 copy-start.3
  4.0 0.7 %copy-done.3 = s32[512]{0:T(512)S(1)} copy-done((s32[512]{0:T(512)S(1)}, s32[512]{0:T(512)}, u32[]{:S(2)}) %copy-start.3) | copy-done | bytes 2072
  4.7 0.0 copy-start.4
  4.7 0.7 %copy-done.4 = s32[512]{0:T(512)S(1)} copy-done((s32[512]{0:T(512)S(1)}, s32[512]{0:T(512)}, u32[]{:S(2)}) %copy-start.4) | copy-done | bytes 2072
  5.4 60.9 %shard_map.64 = bf16[16,2304]{1,0:T(8,128)(2,1)S(1)} custom-call(bf16[512,2304]{1,0:T(8,128)(2,1)S(1)} %copy-done, bf16[512,2304]{1,0:T(8,128)(2,1)S(1)} %copy-done.1, bf16[512,2304]{1,0:T(8,128)(2,1)} %embedding.1, s32[1,512]{1,0:T(1,128)S(1)} %bitcast.5, s32[2,1,256]{2,1,0:T(1,128)S(1)} %bitcast.6, s32[2,1,256]{2,1,0:T(1,128)S(1)} %bitcast.7), custom_call_target="tpu_custom_call" | custom-call | tf_op jit(solution)/shard_map/pallas_call | solution.py:323
  66.3 0.6 copy.8
Async XLA Ops:
  0.0 1.7 %copy-start = (bf16[512,2304]{1,0:T(8,128)(2,1)S(1)}, bf16[512,2304]{1,0:T(8,128)(2,1)}, u32[]{:S(2)}) copy-start(bf16[512,2304]{1,0:T(8,128)(2,1)} %hidden.1) | copy-start | bytes 7077892
  1.7 1.7 %copy-start.1 = (bf16[512,2304]{1,0:T(8,128)(2,1)S(1)}, bf16[512,2304]{1,0:T(8,128)(2,1)}, u32[]{:S(2)}) copy-start(bf16[512,2304]{1,0:T(8,128)(2,1)} %cotangent.1) | copy-start | bytes 7077892
  3.3 0.7 %copy-start.2 = (s32[512]{0:T(512)S(1)}, s32[512]{0:T(512)}, u32[]{:S(2)}) copy-start(s32[512]{0:T(512)} %param.8) | copy-start | bytes 6148
  4.0 0.7 %copy-start.3 = (s32[512]{0:T(512)S(1)}, s32[512]{0:T(512)}, u32[]{:S(2)}) copy-start(s32[512]{0:T(512)} %param.9) | copy-start | bytes 6148
  4.7 0.7 %copy-start.4 = (s32[512]{0:T(512)S(1)}, s32[512]{0:T(512)}, u32[]{:S(2)}) copy-start(s32[512]{0:T(512)} %param.10) | copy-start | bytes 6148

commit v2 on v1

v2 whole, which is shorter than its diff:
```python
import functools
import math

import jax
import jax.numpy as jnp
from jax import lax
from jax.experimental import pallas as pl
from jax.experimental.pallas import tpu as pltpu
from jax.sharding import PartitionSpec as P

D = 4608
SOFTCAP = 30.0
MESH = pl.DeviceIdType.MESH
F32 = jnp.float32
BF16 = jnp.bfloat16
VMEM_LIMIT = 62 * 2**20
PART = 16
CHUNK = 2 * PART
RAW = 2
BLOCKS = ((5, False), (4, False), (5, True), (4, True))


def dot_nt(a, b):
    return lax.dot_general(a, b, (((1,), (1,)), ((), ())), preferred_element_type=F32)


def dot_nn(a, b):
    return lax.dot_general(a, b, (((1,), (0,)), ((), ())), preferred_element_type=F32)


def rows_of(start, size):
    return pl.ds(pl.multiple_of(start, size), size)


def kernel(
    nz, nv, subs, col_x,
    hidden, cotangent, embedding, tokens_in, targets_in, mask_in,
    out,
    tokens, targets, mask, hid, cot, emb, raw_out, raw_in, own, tanhs, shifted, tot_out, tot_in, coeff, sums,
    part_out, part_in, cross_out, cross_in, *rest,
):
    n_subs = len(subs)
    send, recv, sems = rest[:n_subs], rest[n_subs : 2 * n_subs], rest[2 * n_subs :]
    (load, raw_s, raw_r, tot_s, tot_r, ag_s, ag_r, ring_s, ring_r, diag_s, diag_r,
     cross_s, cross_r, part_s, part_r) = sems

    d, v, e = lax.axis_index("dp"), lax.axis_index("vocab"), lax.axis_index("ends")
    z, h = d // 2, d % 2
    steps = nz // 2
    rows, half = own.shape
    width = hid.shape[2]

    def at_z(k, other):
        return (lax.rem(z + k + nz, nz) * 2 + (1 - h if other else h), v, e)

    mate = (d, v, 1 - e)
    across = (z * 2 + 1 - h, v, e)
    ahead = (1, -1)

    quarter = rows // RAW
    other_tokens, own_tokens = rows_of((1 - e) * half, half), rows_of(e * half, half)
    pairs = [(hidden.at[other_tokens], hid.at[1])]
    pairs += [(embedding.at[pl.ds(c * quarter, quarter)], emb.at[pl.ds(c * quarter, quarter)]) for c in range(RAW)]
    pairs += [(hidden.at[own_tokens], hid.at[0]), (tokens_in, tokens), (cotangent, cot), (targets_in, targets), (mask_in, mask)]
    loads = [pltpu.make_async_copy(a, b, load.at[i]) for i, (a, b) in enumerate(pairs)]
    for copy in loads[: RAW + 1]:
        copy.start()

    barrier = pltpu.get_barrier_semaphore()
    greet = [mate, across] + [at_z(k, o) for k in ahead for o in (False, True)]
    greet += [(d, lax.rem(v + o, nv), e) for o in range(1, nv)]
    for who in greet:
        pl.semaphore_signal(barrier, inc=1, device_id=who, device_id_type=MESH)

    def raw_copy(c):
        block = rows_of(c * quarter, quarter)
        return pltpu.make_async_remote_copy(
            src_ref=raw_out.at[block], dst_ref=raw_in.at[block], send_sem=raw_s.at[c], recv_sem=raw_r.at[c],
            device_id=mate, device_id_type=MESH,
        )

    loads[0].wait()
    for c in range(RAW):
        loads[1 + c].wait()
        if c == 0:
            for copy in loads[RAW + 1 :]:
                copy.start()
        block = pl.ds(c * quarter, quarter)
        raw_out[block] = dot_nt(emb[block], hid[1]).astype(BF16)
        if c == 0:
            pl.semaphore_wait(barrier, len(greet))
        raw_copy(c).start()

    loads[RAW + 1].wait()
    for c in range(RAW):
        block = pl.ds(c * quarter, quarter)
        own[block] = dot_nt(emb[block], hid[0])

    for copy in loads[RAW + 2 :]:
        copy.wait()
    normalizer = jnp.asarray(math.sqrt(D), F32).astype(BF16)
    first = v * rows
    fourth = rows // 4

    def embed_block(c, _):
        block = rows_of(c * fourth, fourth)
        index = lax.broadcasted_iota(jnp.int32, (fourth, 2 * half), 0) + (first + c * fourth)
        picks = jnp.where(tokens[...] == index, normalizer.astype(F32), 0.0).astype(BF16)
        third = width // 3 if width % 384 == 0 else width
        for n in range(0, width, third):
            sums[block, pl.ds(n, third)] = dot_nn(picks, cot[:, pl.ds(n, third)])
        return 0

    lax.fori_loop(0, 4, embed_block, 0)

    def soft_block(c, total):
        block = rows_of(c * quarter, quarter)
        raw_copy(c).wait_recv()
        t = jnp.tanh((own[block] + raw_in[block].astype(F32)) * (1.0 / SOFTCAP))
        s = jnp.exp(t * SOFTCAP - SOFTCAP)
        tanhs[block] = t
        shifted[block] = s
        return total + jnp.sum(s, axis=0, keepdims=True)

    total = lax.fori_loop(0, RAW, soft_block, jnp.zeros((1, half), F32))
    tot_out[...] = total

    def tot_copy(o, source):
        return pltpu.make_async_remote_copy(
            src_ref=tot_out, dst_ref=tot_in.at[source], send_sem=tot_s.at[o], recv_sem=tot_r.at[source],
            device_id=(d, lax.rem(v + o, nv), e), device_id_type=MESH,
        )

    for o in range(1, nv):
        tot_copy(o, v).start()
    for o in range(1, nv):
        source = lax.rem(v + o, nv)
        tot_copy(o, source).wait_recv()
        total = total + tot_in[source]
    weight = mask[e].astype(F32)
    target = targets[e]
    inverse = 1.0 / total

    def chunk_at(i):
        s, direction = i // 2, i % 2
        return lax.rem(z + jnp.where(direction == 0, steps - s, steps + s), nz)

    def ag_copy(i):
        block = rows_of(chunk_at(i) * CHUNK, CHUNK)
        return pltpu.make_async_remote_copy(
            src_ref=coeff.at[0, block], dst_ref=coeff.at[1, block], send_sem=ag_s.at[i], recv_sem=ag_r.at[i],
            device_id=mate, device_id_type=MESH,
        )

    def coeff_block(j, _):
        i = jnp.where(j == 0, 0, j + 1)
        start = chunk_at(i) * CHUNK
        block = rows_of(start, CHUNK)
        index = lax.broadcasted_iota(jnp.int32, (CHUNK, half), 0) + (first + start)
        hit = jnp.where(target == index, 1.0, 0.0)
        t = tanhs[block]
        coeff[0, block] = (weight * (shifted[block] * inverse - hit) * (1.0 - t * t)).astype(BF16)
        ag_copy(i).start()
        return 0

    lax.fori_loop(0, nz, coeff_block, 0)

    def complete(chunks, c0, w):
        blocks = [rows_of(c * CHUNK, CHUNK) for c in chunks]
        cols = pl.ds(c0, w)
        got = 0.0
        for k in (0, 1):
            left = coeff[k, blocks[0]] if len(blocks) == 1 else jnp.concatenate([coeff[k, b] for b in blocks], axis=0)
            got = got + dot_nn(left, hid[k, :, cols])
        for i, b in enumerate(blocks):
            sums[b, cols] = sums[b, cols] + got[i * CHUNK : (i + 1) * CHUNK]

    straight_rows, other_rows = rows_of(h * PART, PART), rows_of((1 - h) * PART, PART)

    def ring_copy(direction, u, s, kind):
        source, landing = {
            "full": (pl.ds(0, CHUNK), pl.ds(0, CHUNK)),
            "part": (straight_rows, pl.ds(0, PART)),
            "half": (pl.ds(0, PART), pl.ds(0, PART)),
        }[kind]
        return pltpu.make_async_remote_copy(
            src_ref=send[u].at[direction, s, source], dst_ref=recv[u].at[direction, s, landing],
            send_sem=ring_s.at[direction, u, s], recv_sem=ring_r.at[direction, u, s],
            device_id=at_z(ahead[direction], False), device_id_type=MESH,
        )

    def diag_copy(direction, u):
        s = subs[u][2] - 1
        return pltpu.make_async_remote_copy(
            src_ref=send[u].at[direction, s, other_rows], dst_ref=recv[u].at[direction, s, pl.ds(PART, PART)],
            send_sem=diag_s.at[direction, u], recv_sem=diag_r.at[direction, u],
            device_id=at_z(ahead[direction], True), device_id_type=MESH,
        )

    def cross_copy(direction, s):
        return pltpu.make_async_remote_copy(
            src_ref=cross_out.at[direction, s], dst_ref=cross_in.at[direction, s],
            send_sem=cross_s.at[direction, s], recv_sem=cross_r.at[direction, s],
            device_id=across, device_id_type=MESH,
        )

    part_copy = pltpu.make_async_remote_copy(
        src_ref=part_out, dst_ref=part_in, send_sem=part_s, recv_sem=part_r, device_id=across, device_id_type=MESH,
    )
    cols_x = pl.ds(col_x, width - col_x)

    def row_start(direction, s):
        return chunk_at(2 * s + direction) * CHUNK

    def cross_start(s):
        for direction in (0, 1):
            block = rows_of(row_start(direction, s) + (1 - h) * PART, PART)
            cross_out[direction, s] = sums[block, cols_x].astype(BF16)
            cross_copy(direction, s).start()

    def ring(u, s, direction, fixed):
        c0, w, part = subs[u]
        cols = pl.ds(c0, w)
        start = row_start(direction, s)
        if fixed >= part:
            ring_copy(direction, u, s - 1, "part" if fixed == part else "half").wait_recv()
            got = sums[rows_of(start + h * PART, PART), cols]
            got = got + cross_in[direction, s, :, pl.ds(c0 - col_x, w)].astype(F32)
            got = got + recv[u][direction, s - 1, pl.ds(0, PART)].astype(F32)
            if fixed == part:
                diag_copy(direction, u).wait_recv()
                got = got + recv[u][direction, s - 1, pl.ds(PART, PART)].astype(F32)
            send[u][direction, s, pl.ds(0, PART)] = got.astype(BF16)
            ring_copy(direction, u, s, "half").start()
            return
        got = sums[rows_of(start, CHUNK), cols]
        if fixed > begin(u, direction):
            ring_copy(direction, u, s - 1, "full").wait_recv()
            got = got + recv[u][direction, s - 1].astype(F32)
        send[u][direction, s] = got.astype(BF16)
        if fixed == part - 1:
            diag_copy(direction, u).start()
            ring_copy(direction, u, s, "part").start()
        else:
            ring_copy(direction, u, s, "full").start()

    def begin(u, direction):
        return 0 if direction == u % 2 else 1

    def ag_wait(s, ways=(0, 1)):
        for i in ways:
            ag_copy(2 * s + i).wait_recv()

    def pair(s):
        return [chunk_at(2 * s), chunk_at(2 * s + 1)]

    def iteration(s, fixed):
        later = s + 2
        if fixed < steps - 1:
            ag_wait(later, (0,) if fixed == steps - 2 else (0, 1))
        if fixed >= 2:
            for direction in (0, 1):
                cross_copy(direction, s).wait_recv()
        for u, (c0, w, _) in enumerate(subs):
            for direction in (0, 1):
                if fixed > begin(u, direction):
                    ring(u, s, direction, fixed)
            if fixed < steps - 1:
                complete([z] if fixed == steps - 2 else pair(later), c0, w)
        if fixed < steps - 2:
            cross_start(later)
        if fixed == steps - 2:
            part_out[...] = sums[rows_of(z * CHUNK + (1 - h) * PART, PART)].astype(BF16)
            part_copy.start()

    ag_wait(0, (0,))
    for u, (c0, w, _) in enumerate(subs):
        complete([chunk_at(0)], c0, w)
        ring(u, 0, u % 2, 0)
    ag_wait(1)
    for u, (c0, w, _) in enumerate(subs):
        complete(pair(1), c0, w)
        ring(u, 1, 1 - u % 2, 1)
    ag_wait(2)
    for u, (c0, w, _) in enumerate(subs):
        complete(pair(2), c0, w)
    cross_start(2)

    loop = range(3, steps - 2)
    for s in range(1, steps):
        if s not in loop:
            iteration(s, s)
        elif s == loop[0]:
            def looped(i, _):
                iteration(i, 3)
                return 0

            lax.fori_loop(loop[0], loop[-1] + 1, looped, 0)

    part_copy.wait_recv()
    for u, (c0, w, part) in enumerate(subs):
        cols = pl.ds(c0, w)
        got = sums[rows_of(z * CHUNK + h * PART, PART), cols] + part_in[:, cols].astype(F32)
        for direction in (0, 1):
            ring_copy(direction, u, steps - 1, "part" if part == steps else "half").wait_recv()
            got = got + recv[u][direction, steps - 1, pl.ds(0, PART)].astype(F32)
            if part == steps:
                diag_copy(direction, u).wait_recv()
                got = got + recv[u][direction, steps - 1, pl.ds(PART, PART)].astype(F32)
        out[:, cols] = got.astype(BF16)

    for c in range(RAW):
        raw_copy(c).wait_send()
    for o in range(1, nv):
        tot_copy(o, v).wait_send()
    ag_copy(0).wait_send()

    def ag_done(i, _):
        ag_copy(i).wait_send()
        return 0

    lax.fori_loop(2, 2 * steps + 1, ag_done, 0)
    part_copy.wait_send()
    for direction in (0, 1):
        def cross_done(s, _):
            cross_copy(direction, s).wait_send()
            return 0

        lax.fori_loop(2, steps, cross_done, 0)
    for u, (_, _, part) in enumerate(subs):
        for direction in (0, 1):
            def ring_done(kind, s, _):
                ring_copy(direction, u, s, kind).wait_send()
                return 0

            lax.fori_loop(begin(u, direction), part - 1, functools.partial(ring_done, "full"), 0)
            ring_copy(direction, u, part - 1, "part").wait_send()
            diag_copy(direction, u).wait_send()
            lax.fori_loop(part, steps, functools.partial(ring_done, "half"), 0)


def solution(mesh):
    nz, nv = mesh.shape["dp"] // 2, mesh.shape["vocab"]

    def shards(hidden, cotangent, token_ids, target_ids, loss_mask, embedding):
        tokens, width = hidden.shape
        rows = embedding.shape[0]
        half = tokens // 2
        steps = nz // 2
        shares = sum(share for share, _ in BLOCKS)
        subs, c0 = [], 0
        for share, early in BLOCKS:
            w = width // 128 * share // shares * 128
            subs.append((c0, w, 2 if early else steps))
            c0 += w
        col_x = min(lo for lo, _, part in subs if part == 2)
        any_space = pl.BlockSpec(memory_space=pl.ANY)
        dma = pltpu.SemaphoreType.DMA
        n = len(subs)
        scratch = [
            pltpu.VMEM((1, tokens), jnp.int32),
            pltpu.VMEM((2, 1, half), jnp.int32),
            pltpu.VMEM((2, 1, half), jnp.int32),
            pltpu.VMEM((2, half, width), BF16),
            pltpu.VMEM((tokens, width), BF16),
            pltpu.VMEM((rows, width), BF16),
            pltpu.VMEM((rows, half), BF16),
            pltpu.VMEM((rows, half), BF16),
            pltpu.VMEM((rows, half), F32),
            pltpu.VMEM((rows, half), F32),
            pltpu.VMEM((rows, half), F32),
            pltpu.VMEM((1, half), F32),
            pltpu.VMEM((nv, 1, half), F32),
            pltpu.VMEM((2, rows, half), BF16),
            pltpu.VMEM((rows, width), F32),
            pltpu.VMEM((PART, width), BF16),
            pltpu.VMEM((PART, width), BF16),
            pltpu.VMEM((2, steps, PART, width - col_x), BF16),
            pltpu.VMEM((2, steps, PART, width - col_x), BF16),
        ]
        scratch += [pltpu.VMEM((2, steps, CHUNK, w), BF16) for _, w, _ in subs] * 2
        scratch += [
            dma((RAW + 6,)), dma((RAW,)), dma((RAW,)), dma((nv,)), dma((nv,)),
            dma((2 * steps + 1,)), dma((2 * steps + 1,)),
            dma((2, n, steps)), dma((2, n, steps)), dma((2, n)), dma((2, n)),
            dma((2, steps)), dma((2, steps)), dma, dma,
        ]
        got = pl.pallas_call(
            functools.partial(kernel, nz, nv, subs, col_x),
            out_shape=jax.ShapeDtypeStruct((rows // (2 * nz), width), BF16),
            in_specs=[any_space] * 6,
            out_specs=pl.BlockSpec(memory_space=pltpu.VMEM),
            scratch_shapes=scratch,
            compiler_params=pltpu.CompilerParams(
                collective_id=0, has_side_effects=True, vmem_limit_bytes=VMEM_LIMIT
            ),
        )(
            hidden, cotangent, embedding,
            token_ids.reshape(1, tokens), target_ids.reshape(2, 1, half), loss_mask.reshape(2, 1, half),
        )
        return got[None]

    return jax.shard_map(
        shards,
        mesh=mesh,
        in_specs=(P("dp", "ends"), P("dp", "ends"), P("dp"), P("dp"), P("dp"), P("vocab", "ends")),
        out_specs=P("vocab", "dp", "ends"),
        check_vma=False,
    )
```

time: 67.2 us -> 63.6 us (0.946)
  local copies, waits for them, and re-layouts: 6.01 us -> 1.52 us
  Pallas kernels: 60.9 us -> 61.9 us
    unnamed x11 -> x1, local copies, waits for them, and re-layouts: 6.01 us -> 1.52 us
    pallas_call x1, Pallas kernels: 60.9 us -> 61.9 us  [shards(): pl.pallas_call(functools.partial(kernel, nz, nv, subs, col_x), out_shape=...]
where the time goes in v2:
time: 63.6 us; the launch traced here: 63.4 us
  Pallas kernels  61.9 us (97%)
  local copies, waits for them, and re-layouts  1.52 us (2%)
    pallas_call x1, Pallas kernels, shards(): pl.pallas_call(functools.partial(kernel, nz, nv, subs, col_x), out_shape=...  61.9 us
    unnamed x1, local copies, waits for them, and re-layouts  1.52 us

profile of v2, /device:TPU:2, one launch (start us, length us, event | category | flops | bytes accessed | tf_op | source)
XLA Modules:
  0.0 63.4 jit_solution(9294642371502271656)
XLA Ops:
  0.0 61.9 %shard_map.64 = bf16[16,2304]{1,0:T(8,128)(2,1)} custom-call(bf16[512,2304]{1,0:T(8,128)(2,1)} %hidden.1, bf16[512,2304]{1,0:T(8,128)(2,1)} %cotangent.1, bf16[512,2304]{1,0:T(8,128)(2,1)} %embedding.1, s32[1,512]{1,0:T(1,128)} %bitcast.5, s32[2,1,256]{2,1,0:T(1,128)} %bitcast.6, s32[2,1,256]{2,1,0:T(1,128)} %bitcast.7), custom_call_target="tpu_custom_call" | custom-call | tf_op jit(solution)/shard_map/pallas_call | solution.py:388
  61.9 1.5 %copy.8 = bf16[1,16,2304]{2,1,0:T(8,128)(2,1)} copy(bf16[1,16,2304]{2,1,0:T(8,128)(2,1)} %bitcast.4) | data formatting | bytes 147456

commit v3 on v0

v3 whole, which is shorter than its diff:
```python
import functools
import math

import jax
import jax.numpy as jnp
from jax import lax
from jax.experimental import pallas as pl
from jax.experimental.pallas import tpu as pltpu
from jax.sharding import PartitionSpec as P

D = 4608
SOFTCAP = 30.0
MESH = pl.DeviceIdType.MESH
F32 = jnp.float32
BF16 = jnp.bfloat16
VMEM_LIMIT = 62 * 2**20
PART = 16
CHUNK = 2 * PART
RAW = 4
EARLY = 2
BLOCKS = ((5, False), (4, False), (5, True), (4, True))


def dot_nt(a, b):
    return lax.dot_general(a, b, (((1,), (1,)), ((), ())), preferred_element_type=F32)


def dot_nn(a, b):
    return lax.dot_general(a, b, (((1,), (0,)), ((), ())), preferred_element_type=F32)


def rows_of(start, size):
    return pl.ds(pl.multiple_of(start, size), size)


def kernel(
    nz, nv, subs,
    hidden, cotangent, embedding, tokens_in, targets_in, mask_in,
    out,
    tokens, targets, mask, hid, cot, emb, raw_out, raw_in, own, tilt_out, tilt_in, stats, tot_in, hit_in, sums,
    part_out, part_in, cross_out, cross_in, *rest,
):
    n_subs = len(subs)
    send, recv, sems = rest[:n_subs], rest[n_subs : 2 * n_subs], rest[2 * n_subs :]
    (load, raw_s, raw_r, tot_s, tot_r, tilt_s, tilt_r, hit_s, hit_r, ring_s, ring_r, diag_s, diag_r,
     cross_s, cross_r, part_s, part_r) = sems

    d, v, e = lax.axis_index("dp"), lax.axis_index("vocab"), lax.axis_index("ends")
    z, h = d // 2, d % 2
    steps = nz // 2
    rows, half = own.shape
    width = hid.shape[2]

    def at_z(k, other):
        return (lax.rem(z + k + nz, nz) * 2 + (1 - h if other else h), v, e)

    mate = (d, v, 1 - e)
    across = (z * 2 + 1 - h, v, e)
    ahead = (1, -1)

    def peer(o, f):
        return (d, lax.rem(v + o, nv), (e + f) % 2)

    def chunk_at(place):
        s, direction = (place + 1) // 2, (place + 1) % 2
        return lax.rem(z + (steps - s if direction == 0 or place == 0 else steps + s), nz)

    def place_of(direction, s):
        return 0 if s == 0 else 2 * s - 1 + direction

    def ids_at(place, n):
        return lax.broadcasted_iota(jnp.int32, (CHUNK, n), 0) + (v * rows + chunk_at(place) * CHUNK)

    barrier = pltpu.get_barrier_semaphore()
    greet = [mate, across] + [at_z(k, o) for k in ahead for o in (False, True)] + [at_z(2 * k, False) for k in ahead]
    peers = [(o, f) for o in sorted(range(nv), key=lambda o: -min(o, nv - o)) for f in (1, 0) if (o, f) not in ((0, 0), (0, 1))]
    greet += [peer(o, f) for o, f in peers]
    peers.append((0, 1))
    for who in greet:
        pl.semaphore_signal(barrier, inc=1, device_id=who, device_id_type=MESH)

    quarter = rows // RAW
    per = quarter // CHUNK
    other_tokens, own_tokens = rows_of((1 - e) * half, half), rows_of(e * half, half)
    other_load = pltpu.make_async_copy(hidden.at[other_tokens], hid.at[1], load.at[0])
    other_load.start()
    for place in range(rows // CHUNK):
        pltpu.make_async_copy(
            embedding.at[rows_of(chunk_at(place) * CHUNK, CHUNK)], emb.at[pl.ds(place * CHUNK, CHUNK)],
            load.at[1 + place // per],
        ).start()
    pairs = [(hidden.at[own_tokens], hid.at[0]), (targets_in, targets), (mask_in, mask), (tokens_in, tokens), (cotangent, cot)]
    loads = [pltpu.make_async_copy(a, b, load.at[1 + RAW + i]) for i, (a, b) in enumerate(pairs)]

    def raw_copy(c):
        block = pl.ds(c * quarter, quarter)
        return pltpu.make_async_remote_copy(
            src_ref=raw_out.at[block], dst_ref=raw_in.at[block], send_sem=raw_s.at[c], recv_sem=raw_r.at[c],
            device_id=mate, device_id_type=MESH,
        )

    other_load.wait()
    for c in range(RAW):
        block = pl.ds(c * quarter, quarter)
        pltpu.make_async_copy(embedding.at[block], emb.at[block], load.at[1 + c]).wait()
        raw_out[block] = dot_nt(emb[block], hid[1]).astype(BF16)
        if c == 0:
            pl.semaphore_wait(barrier, len(greet))
        raw_copy(c).start()

    for copy in loads:
        copy.start()
    loads[0].wait()
    for c in range(RAW):
        block = pl.ds(c * quarter, quarter)
        own[block] = dot_nt(emb[block], hid[0])
    loads[1].wait()
    loads[2].wait()

    def tilt_copy(c):
        block = pl.ds(c * quarter, quarter)
        return pltpu.make_async_remote_copy(
            src_ref=tilt_out.at[block], dst_ref=tilt_in.at[block], send_sem=tilt_s.at[c], recv_sem=tilt_r.at[c],
            device_id=mate, device_id_type=MESH,
        )

    def summed(x):
        return jnp.sum(x, axis=0, keepdims=True)

    nothing = jnp.zeros((1, half), F32)
    total, at_shifted, at_slope = nothing, nothing, nothing
    for c in range(RAW):
        raw_copy(c).wait_recv()
        for place in range(c * per, (c + 1) * per):
            block = pl.ds(place * CHUNK, CHUNK)
            t = jnp.tanh((own[block] + raw_in[block].astype(F32)) * (1.0 / SOFTCAP))
            s = jnp.exp(t * SOFTCAP - SOFTCAP)
            slope = 1.0 - t * t
            tilt = s * slope
            own[block] = tilt
            tilt_out[block] = tilt.astype(BF16)
            hit = targets[e] == ids_at(place, half)
            total = total + summed(s)
            at_shifted = at_shifted + summed(jnp.where(hit, s, 0.0))
            at_slope = at_slope + summed(jnp.where(hit, slope, 0.0))
        tilt_copy(c).start()
    stats[0], stats[1], stats[2] = total, at_shifted, at_slope

    def tot_copy(o, f, sent):
        source = (lax.rem(v + o, nv) * 2 + (e + f) % 2) if not sent else v * 2 + e
        return pltpu.make_async_remote_copy(
            src_ref=stats.at[0], dst_ref=tot_in.at[source], send_sem=tot_s.at[o, f], recv_sem=tot_r.at[source],
            device_id=peer(o, f), device_id_type=MESH,
        )

    hit_copy = pltpu.make_async_remote_copy(
        src_ref=stats.at[pl.ds(1, 2)], dst_ref=hit_in, send_sem=hit_s, recv_sem=hit_r, device_id=mate, device_id_type=MESH,
    )
    for o, f in peers:
        tot_copy(o, f, True).start()
    hit_copy.start()
    loads[3].wait()
    loads[4].wait()
    normalizer = jnp.asarray(math.sqrt(D), F32).astype(BF16).astype(F32)
    for c in range(RAW):
        block = pl.ds(c * quarter, quarter)
        picks = [jnp.where(tokens[...] == ids_at(c * per + i, 2 * half), normalizer, 0.0).astype(BF16) for i in range(per)]
        picks = jnp.concatenate(picks, axis=0)
        for c0, w, _ in subs:
            sums[block, pl.ds(c0, w)] = dot_nn(picks, cot[:, pl.ds(c0, w)])

    totals = [total, nothing]
    for o, f in peers:
        tot_copy(o, f, False).wait_recv()
        totals[f] = totals[f] + tot_in[lax.rem(v + o, nv) * 2 + (e + f) % 2]
    hit_copy.wait_recv()
    factors, at_target, wanted = [], [], []
    for f, (a, b) in enumerate(((at_shifted, at_slope), (hit_in[0], hit_in[1]))):
        side = (e + f) % 2
        weight = mask[side].astype(F32)
        inverse = 1.0 / totals[f]
        factors.append(weight * inverse)
        at_target.append(weight * (a * inverse - 1.0) * b)
        wanted.append(targets[side])

    come = []

    def complete(places):
        for c in sorted({place // per for place in places}):
            if c not in come:
                tilt_copy(c).wait_recv()
                come.append(c)
        blocks = [pl.ds(place * CHUNK, CHUNK) for place in places]
        left = []
        for f, tilts in enumerate((own, tilt_in)):
            parts = []
            for place, b in zip(places, blocks):
                hit = wanted[f] == ids_at(place, half)
                parts.append(jnp.where(hit, at_target[f], factors[f] * tilts[b].astype(F32)).astype(BF16))
            left.append(parts[0] if len(parts) == 1 else jnp.concatenate(parts, axis=0))
        for c0, w, _ in subs:
            cols = pl.ds(c0, w)
            got = dot_nn(left[0], hid[0, :, cols]) + dot_nn(left[1], hid[1, :, cols])
            for i, b in enumerate(blocks):
                sums[b, cols] = sums[b, cols] + got[i * CHUNK : (i + 1) * CHUNK]

    straight_rows, other_rows = rows_of(h * PART, PART), rows_of((1 - h) * PART, PART)

    def ring_copy(direction, u, s, kind):
        source, landing = {
            "full": (pl.ds(0, CHUNK), pl.ds(0, CHUNK)),
            "part": (straight_rows, pl.ds(0, PART)),
            "half": (pl.ds(0, PART), pl.ds(0, PART)),
        }[kind]
        return pltpu.make_async_remote_copy(
            src_ref=send[u].at[direction, s, source], dst_ref=recv[u].at[direction, s, landing],
            send_sem=ring_s.at[direction, u, s], recv_sem=ring_r.at[direction, u, s],
            device_id=at_z(ahead[direction] * (2 if s == steps - 2 else 1), False), device_id_type=MESH,
        )

    def diag_copy(direction, u):
        s = subs[u][2] - 1
        return pltpu.make_async_remote_copy(
            src_ref=send[u].at[direction, s, other_rows], dst_ref=recv[u].at[direction, s, pl.ds(PART, PART)],
            send_sem=diag_s.at[direction, u], recv_sem=diag_r.at[direction, u],
            device_id=at_z(ahead[direction], True), device_id_type=MESH,
        )

    def cross_cols(s):
        c0 = min(lo for lo, _, part in subs if part <= s)
        return pl.ds(c0, width - c0)

    def cross_copy(direction, s):
        cols = cross_cols(s)
        return pltpu.make_async_remote_copy(
            src_ref=cross_out.at[direction, s, :, cols], dst_ref=cross_in.at[direction, s, :, cols],
            send_sem=cross_s.at[direction, s], recv_sem=cross_r.at[direction, s],
            device_id=across, device_id_type=MESH,
        )

    part_copy = pltpu.make_async_remote_copy(
        src_ref=part_out, dst_ref=part_in, send_sem=part_s, recv_sem=part_r, device_id=across, device_id_type=MESH,
    )
    def row_start(direction, s):
        return place_of(direction, s) * CHUNK

    def cross_start(s):
        cols = cross_cols(s)
        for direction in (0, 1):
            block = rows_of(row_start(direction, s) + (1 - h) * PART, PART)
            cross_out[direction, s, :, cols] = sums[block, cols].astype(BF16)
            cross_copy(direction, s).start()

    def begin(u, direction):
        return 0 if direction == u % 2 else 1

    def ring(u, s, direction):
        c0, w, part = subs[u]
        cols = pl.ds(c0, w)
        start = row_start(direction, s)
        if s >= part:
            got = sums[rows_of(start + h * PART, PART), cols] + cross_in[direction, s, :, cols].astype(F32)
            if begin(u, direction) < s < steps - 1:
                ring_copy(direction, u, s - 1, "part" if s == part else "half").wait_recv()
                got = got + recv[u][direction, s - 1, pl.ds(0, PART)].astype(F32)
                if s == part:
                    diag_copy(direction, u).wait_recv()
                    got = got + recv[u][direction, s - 1, pl.ds(PART, PART)].astype(F32)
            send[u][direction, s, pl.ds(0, PART)] = got.astype(BF16)
            ring_copy(direction, u, s, "half").start()
            return
        got = sums[pl.ds(start, CHUNK), cols]
        if s > begin(u, direction):
            ring_copy(direction, u, s - 1, "full").wait_recv()
            got = got + recv[u][direction, s - 1].astype(F32)
        send[u][direction, s] = got.astype(BF16)
        if s == part - 1:
            diag_copy(direction, u).start()
            ring_copy(direction, u, s, "part").start()
        else:
            ring_copy(direction, u, s, "full").start()

    def pair(s):
        return [place_of(0, s), place_of(1, s)]

    def cross_wait(s):
        for direction in (0, 1):
            cross_copy(direction, s).wait_recv()

    def sent(s):
        for direction in (0, 1):
            if s >= EARLY:
                cross_copy(direction, s).wait_send()
            for u, (_, _, part) in enumerate(subs):
                if s >= begin(u, direction):
                    kind = "full" if s < part - 1 else "part" if s == part - 1 else "half"
                    ring_copy(direction, u, s, kind).wait_send()
                    if kind == "part":
                        diag_copy(direction, u).wait_send()

    complete([0])
    for u in range(n_subs):
        ring(u, 0, u % 2)
    complete(pair(1))
    if EARLY == 1:
        cross_start(1)
    for u, (_, _, part) in enumerate(subs):
        if part > 1:
            ring(u, 1, 1 - u % 2)
    complete(pair(2))
    if EARLY <= 2:
        cross_start(2)
    if EARLY == 1:
        cross_wait(1)
        for u, (_, _, part) in enumerate(subs):
            if part == 1:
                ring(u, 1, 1 - u % 2)
    for s in range(1, steps - 1):
        if s >= EARLY:
            cross_wait(s)
        for u in range(n_subs):
            for direction in (0, 1):
                if s > begin(u, direction):
                    ring(u, s, direction)
        if s < steps - 2:
            complete(pair(s + 2))
            if s + 2 >= EARLY:
                cross_start(s + 2)
        if s == steps - 3:
            complete([2 * steps - 1])
            part_out[...] = sums[rows_of((2 * steps - 1) * CHUNK + (1 - h) * PART, PART)].astype(BF16)
            part_copy.start()
        if s == 1:
            for c in range(RAW):
                raw_copy(c).wait_send()
                tilt_copy(c).wait_send()
            for o, f in peers:
                tot_copy(o, f, True).wait_send()
            hit_copy.wait_send()
        else:
            sent(s - 2)
    cross_wait(steps - 1)
    for u in range(n_subs):
        for direction in (0, 1):
            ring(u, steps - 1, direction)
    sent(steps - 3)

    part_copy.wait_recv()
    for u, (c0, w, part) in enumerate(subs):
        cols = pl.ds(c0, w)
        got = sums[rows_of((2 * steps - 1) * CHUNK + h * PART, PART), cols] + part_in[:, cols].astype(F32)
        for direction in (0, 1):
            for s in (steps - 2, steps - 1):
                ring_copy(direction, u, s, "half").wait_recv()
                got = got + recv[u][direction, s, pl.ds(0, PART)].astype(F32)
        out[:, cols] = got.astype(BF16)

    sent(steps - 2)
    sent(steps - 1)
    part_copy.wait_send()


def solution(mesh):
    nz, nv = mesh.shape["dp"] // 2, mesh.shape["vocab"]

    def shards(hidden, cotangent, token_ids, target_ids, loss_mask, embedding):
        tokens, width = hidden.shape
        rows = embedding.shape[0]
        half = tokens // 2
        steps = nz // 2
        shares = sum(share for share, _ in BLOCKS)
        subs, c0 = [], 0
        for share, early in BLOCKS:
            w = width // 128 * share // shares * 128
            subs.append((c0, w, EARLY if early else steps - 2))
            c0 += w
        any_space = pl.BlockSpec(memory_space=pl.ANY)
        dma = pltpu.SemaphoreType.DMA
        n = len(subs)
        scratch = [
            pltpu.VMEM((1, tokens), jnp.int32),
            pltpu.VMEM((2, 1, half), jnp.int32),
            pltpu.VMEM((2, 1, half), jnp.int32),
            pltpu.VMEM((2, half, width), BF16),
            pltpu.VMEM((tokens, width), BF16),
            pltpu.VMEM((rows, width), BF16),
            pltpu.VMEM((rows, half), BF16),
            pltpu.VMEM((rows, half), BF16),
            pltpu.VMEM((rows, half), F32),
            pltpu.VMEM((rows, half), BF16),
            pltpu.VMEM((rows, half), BF16),
            pltpu.VMEM((3, 1, half), F32),
            pltpu.VMEM((2 * nv, 1, half), F32),
            pltpu.VMEM((2, 1, half), F32),
            pltpu.VMEM((rows, width), F32),
            pltpu.VMEM((PART, width), BF16),
            pltpu.VMEM((PART, width), BF16),
            pltpu.VMEM((2, steps, PART, width), BF16),
            pltpu.VMEM((2, steps, PART, width), BF16),
        ]
        scratch += [pltpu.VMEM((2, steps, CHUNK, w), BF16) for _, w, _ in subs] * 2
        scratch += [
            dma((RAW + 6,)), dma((RAW,)), dma((RAW,)), dma((nv, 2)), dma((2 * nv,)),
            dma((RAW,)), dma((RAW,)), dma, dma,
            dma((2, n, steps)), dma((2, n, steps)), dma((2, n)), dma((2, n)),
            dma((2, steps)), dma((2, steps)), dma, dma,
        ]
        got = pl.pallas_call(
            functools.partial(kernel, nz, nv, subs),
            out_shape=jax.ShapeDtypeStruct((rows // (2 * nz), width), BF16),
            in_specs=[any_space] * 6,
            out_specs=pl.BlockSpec(memory_space=pltpu.VMEM),
            scratch_shapes=scratch,
            compiler_params=pltpu.CompilerParams(
                collective_id=0, has_side_effects=True, vmem_limit_bytes=VMEM_LIMIT
            ),
        )(
            hidden, cotangent, embedding,
            token_ids.reshape(1, tokens), target_ids.reshape(2, 1, half), loss_mask.reshape(2, 1, half),
        )
        return got[None]

    return jax.shard_map(
        shards,
        mesh=mesh,
        in_specs=(P("dp", "ends"), P("dp", "ends"), P("dp"), P("dp"), P("dp"), P("vocab", "ends")),
        out_specs=P("vocab", "dp", "ends"),
        check_vma=False,
    )
```

time: 777 us -> 61.9 us (0.08)
  the two profiles are of different devices: /device:TPU:8 before, /device:TPU:2 now
where the time goes in v3:
time: 61.9 us; the launch traced here: 61.8 us
  Pallas kernels  60.2 us (97%)
  local copies, waits for them, and re-layouts  1.52 us (2%)
    pallas_call x1, Pallas kernels, shards(): pl.pallas_call(functools.partial(kernel, nz, nv, subs), out_shape=jax.Sha...  60.2 us
    unnamed x1, local copies, waits for them, and re-layouts  1.52 us

profile of v3, /device:TPU:2, one launch (start us, length us, event | category | flops | bytes accessed | tf_op | source)
XLA Modules:
  0.0 61.8 jit_solution(3913445967834833870)
XLA Ops:
  0.0 60.2 %shard_map.64 = bf16[16,2304]{1,0:T(8,128)(2,1)} custom-call(bf16[512,2304]{1,0:T(8,128)(2,1)} %hidden.1, bf16[512,2304]{1,0:T(8,128)(2,1)} %cotangent.1, bf16[512,2304]{1,0:T(8,128)(2,1)} %embedding.1, s32[1,512]{1,0:T(1,128)} %bitcast.5, s32[2,1,256]{2,1,0:T(1,128)} %bitcast.6, s32[2,1,256]{2,1,0:T(1,128)} %bitcast.7), custom_call_target="tpu_custom_call" | custom-call | tf_op jit(solution)/shard_map/pallas_call | solution.py:408
  60.2 1.5 %copy.8 = bf16[1,16,2304]{2,1,0:T(8,128)(2,1)} copy(bf16[1,16,2304]{2,1,0:T(8,128)(2,1)} %bitcast.4) | data formatting | bytes 147456

commit v4 on v3

--- a/solution.py
+++ b/solution.py
@@ -307,9 +307,10 @@
     for u, (_, _, part) in enumerate(subs):
         if part > 1:
             ring(u, 1, 1 - u % 2)
-    complete(pair(2))
-    if EARLY <= 2:
-        cross_start(2)
+    for s in (2, 3):
+        complete(pair(s))
+        if s >= EARLY:
+            cross_start(s)
     if EARLY == 1:
         cross_wait(1)
         for u, (_, _, part) in enumerate(subs):
@@ -322,11 +323,15 @@
             for direction in (0, 1):
                 if s > begin(u, direction):
                     ring(u, s, direction)
-        if s < steps - 2:
-            complete(pair(s + 2))
-            if s + 2 >= EARLY:
-                cross_start(s + 2)
+        if s < steps - 3:
+            complete(pair(s + 3))
+            if s + 3 >= EARLY:
+                cross_start(s + 3)
         if s == steps - 3:
+            cross_wait(steps - 1)
+            for u in range(n_subs):
+                for direction in (0, 1):
+                    ring(u, steps - 1, direction)
             complete([2 * steps - 1])
             part_out[...] = sums[rows_of((2 * steps - 1) * CHUNK + (1 - h) * PART, PART)].astype(BF16)
             part_copy.start()
@@ -339,10 +344,6 @@
             hit_copy.wait_send()
         else:
             sent(s - 2)
-    cross_wait(steps - 1)
-    for u in range(n_subs):
-        for direction in (0, 1):
-            ring(u, steps - 1, direction)
     sent(steps - 3)
 
     part_copy.wait_recv()

time: 61.9 us -> 60.3 us (0.974)
  the two profiles are of different devices: /device:TPU:2 before, /device:TPU:8 now
where the time goes in v4:
time: 60.3 us; the launch traced here: 60.1 us
  Pallas kernels  58.6 us (97%)
  local copies, waits for them, and re-layouts  1.52 us (3%)
    pallas_call x1, Pallas kernels, shards(): pl.pallas_call(functools.partial(kernel, nz, nv, subs), out_shape=jax.Sha...  58.6 us
    unnamed x1, local copies, waits for them, and re-layouts  1.52 us

profile of v4, /device:TPU:8, one launch (start us, length us, event | category | flops | bytes accessed | tf_op | source)
XLA Modules:
  0.0 60.1 jit_solution(18237031756496466630)
XLA Ops:
  0.0 58.6 %shard_map.64 = bf16[16,2304]{1,0:T(8,128)(2,1)} custom-call(bf16[512,2304]{1,0:T(8,128)(2,1)} %hidden.1, bf16[512,2304]{1,0:T(8,128)(2,1)} %cotangent.1, bf16[512,2304]{1,0:T(8,128)(2,1)} %embedding.1, s32[1,512]{1,0:T(1,128)} %bitcast.5, s32[2,1,256]{2,1,0:T(1,128)} %bitcast.6, s32[2,1,256]{2,1,0:T(1,128)} %bitcast.7), custom_call_target="tpu_custom_call" | custom-call | tf_op jit(solution)/shard_map/pallas_call | solution.py:409
  58.6 1.5 %copy.8 = bf16[1,16,2304]{2,1,0:T(8,128)(2,1)} copy(bf16[1,16,2304]{2,1,0:T(8,128)(2,1)} %bitcast.4) | data formatting | bytes 147456

commit v5 on v4

--- a/solution.py
+++ b/solution.py
@@ -143,7 +143,8 @@
             total = total + summed(s)
             at_shifted = at_shifted + summed(jnp.where(hit, s, 0.0))
             at_slope = at_slope + summed(jnp.where(hit, slope, 0.0))
-        tilt_copy(c).start()
+        if c < RAW - 1:
+            tilt_copy(c).start()
     stats[0], stats[1], stats[2] = total, at_shifted, at_slope
 
     def tot_copy(o, f, sent):
@@ -159,6 +160,7 @@
     for o, f in peers:
         tot_copy(o, f, True).start()
     hit_copy.start()
+    tilt_copy(RAW - 1).start()
     loads[3].wait()
     loads[4].wait()
     normalizer = jnp.asarray(math.sqrt(D), F32).astype(BF16).astype(F32)

time: 60.3 us -> 59.2 us (0.982)
  the two profiles are of different devices: /device:TPU:8 before, /device:TPU:34 now
where the time goes in v5:
time: 59.2 us; the launch traced here: 59.1 us
  Pallas kernels  57.5 us (97%)
  local copies, waits for them, and re-layouts  1.52 us (3%)
    pallas_call x1, Pallas kernels, shards(): pl.pallas_call(functools.partial(kernel, nz, nv, subs), out_shape=jax.Sha...  57.5 us
    unnamed x1, local copies, waits for them, and re-layouts  1.52 us

profile of v5, /device:TPU:34, one launch (start us, length us, event | category | flops | bytes accessed | tf_op | source)
XLA Modules:
  0.0 59.1 jit_solution(8889578624039312657)
XLA Ops:
  0.0 57.5 %shard_map.64 = bf16[16,2304]{1,0:T(8,128)(2,1)} custom-call(bf16[512,2304]{1,0:T(8,128)(2,1)} %hidden.1, bf16[512,2304]{1,0:T(8,128)(2,1)} %cotangent.1, bf16[512,2304]{1,0:T(8,128)(2,1)} %embedding.1, s32[1,512]{1,0:T(1,128)} %bitcast.5, s32[2,1,256]{2,1,0:T(1,128)} %bitcast.6, s32[2,1,256]{2,1,0:T(1,128)} %bitcast.7), custom_call_target="tpu_custom_call" | custom-call | tf_op jit(solution)/shard_map/pallas_call | solution.py:411
  57.6 1.5 %copy.8 = bf16[1,16,2304]{2,1,0:T(8,128)(2,1)} copy(bf16[1,16,2304]{2,1,0:T(8,128)(2,1)} %bitcast.4) | data formatting | bytes 147456
